TPU v7x, 256 devices: a whole 4x4x8 slice. The times are simulated.
256 devices in a mesh: seq: 16 (over z, y_lo), row: 2 (over y_hi), col: 8 (over x, core).
Axes of the slice: x: 4, y: 4 (y_hi: 2, y_lo: 2; y = y_hi * 2 + y_lo), z: 8, core: 2. Of those that a mesh axis runs over, the one named last changes fastest.
Arguments:
- tokens: bfloat16 [8192, 4096], P(('seq', 'row'), 'col'), may hold values from -20 to 20
- w_query: bfloat16 [4096, 2048], P('row', 'col'), may hold values from -1 to 1
- w_key: bfloat16 [4096, 2048], P('row', 'col'), may hold values from -1 to 1
- w_value: bfloat16 [4096, 2048], P('row', 'col'), may hold values from -0.09375 to 0.09375
- w_out: bfloat16 [2048, 4096], P('row', 'col'), may hold values from -0.125 to 0.125
Outputs:
- mixed: bfloat16 [8192, 4096], P(('seq', 'row'), 'col')
All inputs are finite; a program needn't handle non-finite values.
Results may differ from a plain program's by a relative error of at most 0.01125.
Values may be sent and summed in bfloat16 or wider, within the bound.
A program may use at most 64 MiB of HBM per device.

v0:
```python
import math

import jax
import jax.numpy as jnp
from jax import lax
from jax.experimental import pallas as pl
from jax.experimental.pallas import tpu as pltpu
from jax.sharding import PartitionSpec as P

HEAD_DIM = 64
F32 = jnp.float32
BF16 = jnp.bfloat16


def dot_t(a, b):
    return lax.dot_general(a, b, (((1,), (1,)), ((), ())), preferred_element_type=F32)


def dot(a, b):
    return jnp.dot(a, b, preferred_element_type=F32)


def kernel(
    tok, wq, wk, wv, wo, out,
    tokbuf, wbuf, wobuf, qf, pf, ps, pr, kvb, qb, mst, acc, ao, att, lhs,
    wsem, locsem, tsem, trsem, tsib, tsibr, psem, prsem, rsem, rrsem,
    wosem, worsem, fsem, arsem, asib, asibr,
):
    seq, yh, col = lax.axis_index("seq"), lax.axis_index("row"), lax.axis_index("col")
    z, yl = seq // 2, seq % 2
    x, k = col // 2, col % 2
    xp = x % 2
    hx = x // 2
    y = yh * 2 + yl
    src = 1 - (hx - yh) * (hx - yh)
    is_src, is_sink = src == 1, src == 0

    def dev(seq=seq, row=yh, col=col):
        return {"seq": seq, "row": row, "col": col}

    xs = [x, x + 1 - 2 * xp, 3 - x, (x + 2) % 4]
    ys = [(yl, yh), (1 - yl, 1 - yh), (1 - yl, yh), (yl, 1 - yh)]

    def at(b, i):
        return dev(seq=z * 2 + ys[b][0], row=ys[b][1], col=xs[i] * 2 + k)

    sib = dev(col=x * 2 + 1 - k)
    part, ysw = at(1, 0), at(2, 0)
    zr = dev(seq=((z + 1) % 8) * 2 + yl)
    zl = dev(seq=((z + 7) % 8) * 2 + yl)

    def rc(s, d, ss, rs, to):
        return pltpu.make_async_remote_copy(
            src_ref=s, dst_ref=d, send_sem=ss, recv_sem=rs, device_id=to,
            device_id_type=pl.DeviceIdType.MESH,
        )

    sent = {"all": [], "src": [], "sink": []}

    def go(who, make, *args):
        make(*args).start()
        sent[who].append((make, args))

    def finish():
        for make, args in sent["all"]:
            make(*args).wait_send()

        @pl.when(is_src)
        def _():
            for make, args in sent["src"]:
                make(*args).wait_send()

        @pl.when(is_sink)
        def _():
            for make, args in sent["sink"]:
                make(*args).wait_send()

        for pending in sent.values():
            pending.clear()

    wloads = [
        pltpu.make_async_copy(w, wbuf.at[i], wsem.at[i]) for i, w in enumerate((wq, wk, wv))
    ]
    own_half = pl.ds(pl.multiple_of(yh * 1024, 1024), 1024)
    wloads.append(pltpu.make_async_copy(wo, wobuf.at[own_half, :], wsem.at[3]))
    for w in wloads:
        w.start()
    own_f = xp * 2 + k

    def tsrc(c):
        return tok.at[pl.ds(c * 128, 128), :]

    def tslot(c, f, a):
        return tokbuf.at[c, f, pl.ds(pl.multiple_of(a * 128, 128), 128), :]

    def tload(c):
        return pltpu.make_async_copy(tsrc(c), tslot(c, own_f, yh), locsem.at[c])

    @pl.when(is_src)
    def _():
        for c in range(2):
            tload(c).start()

    barrier = pltpu.get_barrier_semaphore()
    for to in [sib, zr, zl] + [at(b, i) for b in range(4) for i in range(4) if b + i > 0]:
        pl.semaphore_signal(barrier, inc=1, device_id=to, device_id_type=pl.DeviceIdType.MESH)
    pl.semaphore_wait(barrier, 18)

    def tcopy(c, b, i):
        return rc(tsrc(c), tslot(c, own_f, yh), tsem.at[c, i], trsem.at[c, own_f, yh], at(b, i))

    def twait(c, f, a):
        slot = tslot(c, f, a)
        rc(slot, slot, tsem.at[c, 0], trsem.at[c, f, a], sib).wait_recv()

    def tsibc(c, f, a):
        slot = tslot(c, f, a)
        return rc(slot, slot, tsib.at[c, f // 2, a], tsibr.at[c, f, a], sib)

    def tsib0(c):
        return rc(
            tsrc(c), tslot(c, own_f, yh), tsib.at[c, own_f // 2, yh], tsibr.at[c, own_f, yh], sib
        )

    @pl.when(is_src)
    def _():
        for c in range(2):
            for i in (3, 1, 2):
                go("src", tcopy, c, 0, i)
            go("src", tsib0, c)

    @pl.when(is_sink)
    def _():
        for c in range(2):
            for i in (3, 1, 2, 0):
                go("sink", tcopy, c, 1, i)
    f_other = (1 - xp) * 2 + k
    not_k = 1 - k

    def pass_on(c):
        twait(c, f_other, yh)
        go("all", tsibc, c, f_other, yh)

        @pl.when(is_src)
        def _():
            tload(c).wait()

        @pl.when(is_sink)
        def _():
            twait(c, own_f, yh)
            go("sink", tsibc, c, own_f, yh)

        for f in (own_f, f_other):
            twait(c, f, 1 - yh)
            go("all", tsibc, c, f, 1 - yh)

    def from_sib(c):
        for f in (xp * 2 + not_k, (1 - xp) * 2 + not_k):
            for a in range(2):
                slot = tslot(c, f, a)
                rc(slot, slot, tsib.at[c, 0, 0], tsibr.at[c, f, a], sib).wait_recv()

    low = lax.broadcasted_iota(jnp.int32, (256, 128), 1) < 64
    qscale = math.log2(math.e) / HEAD_DIM**0.5

    def pcopy(s, b):
        j = ys[b][1] * 2 + ys[b][0]
        return rc(ps.at[s, j], pr.at[s, b], psem.at[s, b], prsem.at[s, b], at(b, 0))

    def product(c, i):
        full = dot(tokbuf[c, 0], wbuf[i, 0:512, :])
        for f in range(1, 4):
            full += dot(tokbuf[c, f], wbuf[i, f * 512 : (f + 1) * 512, :])
        return full

    def pair_up(s, left, right):
        for h in range(2):
            lt, rt = left[:, h * 128 : h * 128 + 128], right[:, h * 128 : h * 128 + 128]
            even = jnp.where(low, lt, pltpu.roll(rt, 64, 1))
            odd = jnp.where(low, pltpu.roll(lt, 64, 1), rt)
            pf[s, 2 * h], pf[s, 2 * h + 1] = even, odd
            ps[s, 2 * h], ps[s, 2 * h + 1] = even.astype(BF16), odd.astype(BF16)
        for b in (3, 1, 2):
            go("all", pcopy, s, b)

    def whole(s, g):
        if g == 0:
            pcopy(s, 1).wait_recv()
            return pf[s, y] + pr[s, 1].astype(F32)
        pcopy(s, 2).wait_recv()
        pcopy(s, 3).wait_recv()
        return pr[s, 2].astype(F32) + pr[s, 3].astype(F32)

    def slots(i):
        t = i + 1
        d = (t + 1) // 2
        g_r = (t + 1) % 2
        ends = t // 7 + (7 - t) // 7
        g_l = g_r + ends * (1 - 2 * g_r)
        return (z - d + 8) % 8, g_r, (z + d) % 8, g_l

    def ring(way, i, zs, g):
        ref = kvb.at[zs, g]
        return rc(ref, ref, rsem.at[way, i], rrsem.at[way, i], (zr, zl)[way])

    def wcopy(t):
        return rc(
            wo.at[t * 128 : t * 128 + 128, :],
            wobuf.at[pl.ds(pl.multiple_of(yh * 1024 + t * 128, 128), 128), :],
            wosem.at[t], worsem.at[t], part,
        )

    pass_on(0)
    for w in wloads:
        w.wait()
    from_sib(0)
    pair_up(0, product(0, 1), product(0, 2))
    qf[...] = product(0, 0)
    pass_on(1)
    from_sib(1)
    pair_up(1, product(1, 1), product(1, 2))
    qfull = product(1, 0)
    for h in range(2):
        lt, rt = qf[:, h * 128 : h * 128 + 128], qfull[:, h * 128 : h * 128 + 128]
        even = jnp.where(low, lt, pltpu.roll(rt, 64, 1))
        odd = jnp.where(low, pltpu.roll(lt, 64, 1), rt)
        pf[2, 2 * h], pf[2, 2 * h + 1] = even, odd
        ps[2, 2 * h], ps[2, 2 * h + 1] = even.astype(BF16), odd.astype(BF16)
    for b in (3, 1, 2):
        go("all", pcopy, 2, b)
    mst[...] = jnp.full_like(mst, -1e30)
    acc[...] = jnp.zeros_like(acc)
    for t in range(8):
        go("all", wcopy, t)
    for g in range(2):
        for c in range(2):
            kvb[z, g, c * 256 : c * 256 + 256, :] = whole(c, g).astype(BF16)
        for way in (0, 1):
            go("all", ring, way, g, z, g)
    for g in range(2):
        q = whole(2, g) * qscale
        qb[g * 512 : g * 512 + 256, :] = jnp.where(low, q, 0.0).astype(BF16)
        qb[g * 512 + 256 : g * 512 + 512, :] = jnp.where(low, pltpu.roll(q, 64, 1), 0.0).astype(BF16)

    def step(t, carry):
        i = t - 1
        z_r, g_r, z_l, g_l = slots(i)

        @pl.when(t >= 1)
        def _():
            ring(0, i, z_r, g_r).wait_recv()

            @pl.when(i <= 4)
            def _():
                ring(0, i + 2, z_r, g_r).start()

            ring(1, i, z_l, g_l).wait_recv()

            @pl.when(i <= 3)
            def _():
                ring(1, i + 2, z_l, g_l).start()

            @pl.when(i == 5)
            def _():
                ring(1, i + 1, z_l, g_l).start()

        kv = jnp.concatenate([kvb[z_r, g_r], kvb[z_l, g_l]], axis=0)
        lane = lax.broadcasted_iota(jnp.int32, kv.shape, 1)
        vals = jnp.where(lane < 64, jnp.ones_like(kv), kv)
        s = dot_t(qb[...], kv)
        n = s.shape[1] // 128
        old = mst[...]
        mx = s[:, :128]
        for j in range(1, n):
            mx = jnp.maximum(mx, s[:, j * 128 : (j + 1) * 128])
        new = jnp.maximum(old, jnp.max(mx, axis=1, keepdims=True))
        w = jnp.concatenate(
            [jnp.exp2(s[:, j * 128 : (j + 1) * 128] - new).astype(BF16) for j in range(n)], axis=1
        )
        acc[...] = acc[...] * jnp.exp2(old - new) + dot(w, vals)
        mst[...] = new
        return carry

    lax.fori_loop(0, 8, step, 0)
    for way in (0, 1):
        for i in range(2, 7):
            sent["all"].append((ring, (way, i, z, 0)))

    early = {who: pending[:] for who, pending in sent.items()}
    for pending in sent.values():
        pending.clear()
    low2 = lax.broadcasted_iota(jnp.int32, (128, 128), 1) < 64

    def hand(b, i):
        return rc(ao.at[b], att.at[col, y], fsem.at[b, i], arsem.at[col, y], at(b, i))

    for b in (3, 1, 2, 0):
        g, a = b // 2, ys[b][1]
        r0 = pl.multiple_of(g * 512 + a * 128, 128)
        t0 = acc[pl.ds(r0, 128), :]
        t1 = acc[pl.ds(r0 + 256, 128), :]
        o0 = t0 / pltpu.roll(t0, 64, 1)
        o1 = t1 / pltpu.roll(t1, 64, 1)
        packed = jnp.where(low2, pltpu.roll(o0, 64, 1), o1).astype(BF16)
        ao[b] = packed
        if b == 0:
            att[col, y] = packed
        for i in (3, 1, 2, 0):
            if b + i > 0:
                go("all", hand, b, i)

    handed = sent["all"][:]
    for who, pending in early.items():
        sent[who][:] = pending
    finish()
    sent["all"][:] = handed

    def acopy(q):
        c8 = xs[q] * 2 + k
        return rc(att.at[c8], att.at[c8], asib.at[q], asibr.at[c8], sib)

    for q in range(4):
        for b in range(4):
            if q + b > 0:
                ref = att.at[xs[q] * 2 + k, ys[b][1] * 2 + ys[b][0]]
                rc(ref, ref, fsem.at[0, 0], arsem.at[xs[q] * 2 + k, ys[b][1] * 2 + ys[b][0]], sib).wait_recv()
        go("all", acopy, q)
    for t in range(8):
        there = pl.ds(pl.multiple_of((1 - yh) * 1024 + t * 128, 128), 128)
        rc(wobuf.at[there, :], wobuf.at[there, :], wosem.at[t], worsem.at[t], sib).wait_recv()

    total = None
    for q in range(4):
        c8 = xs[q] * 2 + 1 - k
        rc(att.at[c8], att.at[c8], asib.at[q], asibr.at[c8], sib).wait_recv()
        for kk in range(2):
            for p in range(2):
                b0, b1 = att[xs[q] * 2 + kk, 2 * p], att[xs[q] * 2 + kk, 2 * p + 1]
                c0 = kk * 256 + p * 128
                lhs[q, 0:128, c0 : c0 + 128] = jnp.concatenate([b0[:, :64], b1[:, :64]], axis=1)
                lhs[q, 128:256, c0 : c0 + 128] = jnp.concatenate([b0[:, 64:], b1[:, 64:]], axis=1)
        term = dot(lhs[q], wobuf[pl.ds(pl.multiple_of(xs[q] * 512, 512), 512), :])
        total = term if total is None else total + term
    out[...] = total.astype(BF16)
    finish()


def on_device(tokens, w_query, w_key, w_value, w_out):
    dma = pltpu.SemaphoreType.DMA
    scratch = [
        pltpu.VMEM((2, 4, 256, 512), BF16),
        pltpu.VMEM((3, 2048, 256), BF16),
        pltpu.VMEM((2048, 512), BF16),
        pltpu.VMEM((256, 256), F32),
        pltpu.VMEM((3, 4, 256, 128), F32),
        pltpu.VMEM((3, 4, 256, 128), BF16),
        pltpu.VMEM((3, 4, 256, 128), BF16),
        pltpu.VMEM((8, 2, 512, 128), BF16),
        pltpu.VMEM((1024, 128), BF16),
        pltpu.VMEM((1024, 128), F32),
        pltpu.VMEM((1024, 128), F32),
        pltpu.VMEM((4, 128, 128), BF16),
        pltpu.VMEM((8, 4, 128, 128), BF16),
        pltpu.VMEM((4, 256, 512), BF16),
        dma((4,)), dma((2,)), dma((2, 4)), dma((2, 4, 2)), dma((2, 2, 2)), dma((2, 4, 2)),
        dma((3, 4)), dma((3, 4)), dma((2, 7)), dma((2, 7)),
        dma((8,)), dma((8,)), dma((4, 4)), dma((8, 4)), dma((4,)), dma((8,)),
    ]
    return pl.pallas_call(
        kernel,
        out_shape=jax.ShapeDtypeStruct((256, 512), BF16),
        in_specs=[pl.BlockSpec(memory_space=pl.ANY)] * 5,
        out_specs=pl.BlockSpec(memory_space=pltpu.VMEM),
        scratch_shapes=scratch,
        compiler_params=pltpu.CompilerParams(
            collective_id=0, has_side_effects=True, vmem_limit_bytes=54848 << 10
        ),
    )(tokens, w_query, w_key, w_value, w_out)


def solution(mesh):
    in_specs = (
        P(("seq", "row"), "col"),
        P("row", "col"),
        P("row", "col"),
        P("row", "col"),
        P("row", "col"),
    )
    out_specs = P(("seq", "row"), "col")
    return jax.shard_map(
        on_device, mesh=mesh, in_specs=in_specs, out_specs=out_specs, check_vma=False
    )
```

profile of v0, /device:TPU:1, one launch (start us, length us, event | category | flops | bytes accessed | tf_op | source)
XLA Modules:
  0.0 68.1 jit_solution(8126001978484306930)
XLA Ops:
  0.0 67.4 %shard_map.55 = bf16[256,512]{1,0:T(8,128)(2,1)S(1)} custom-call(bf16[256,512]{1,0:T(8,128)(2,1)} %tok.1, bf16[2048,256]{1,0:T(8,128)(2,1)} %wq.1, bf16[2048,256]{1,0:T(8,128)(2,1)} %wk.1, bf16[2048,256]{1,0:T(8,128)(2,1)} %wv.1, bf16[1024,512]{1,0:T(8,128)(2,1)} %wo.1), custom_call_target="tpu_custom_call" | custom-call | tf_op jit(solution)/shard_map/pallas_call | solution.py:369
  67.4 0.7 %copy.7 = bf16[256,512]{1,0:T(8,128)(2,1)} copy(bf16[256,512]{1,0:T(8,128)(2,1)S(1)} %shard_map.55) | data formatting | bytes 524288
where the time goes:
time: 68.2 us; the launch traced here: 68.1 us
  Pallas kernels  67.4 us (99%)
  local copies, waits for them, and re-layouts  0.71 us (1%)
    pallas_call x1, Pallas kernels, on_device(): pl.pallas_call(kernel, out_shape=jax.ShapeDtypeStruct((256, 512), BF16),...  67.4 us

commit v1 on v0

--- a/solution.py
+++ b/solution.py
@@ -8,6 +8,7 @@
 from jax.sharding import PartitionSpec as P
 
 HEAD_DIM = 64
+AHEAD = 3
 F32 = jnp.float32
 BF16 = jnp.bfloat16
 
@@ -199,9 +200,9 @@
         g_l = g_r + ends * (1 - 2 * g_r)
         return (z - d + 8) % 8, g_r, (z + d) % 8, g_l
 
-    def ring(way, i, zs, g):
-        ref = kvb.at[zs, g]
-        return rc(ref, ref, rsem.at[way, i], rrsem.at[way, i], (zr, zl)[way])
+    def ring(way, i, c, zs, g):
+        ref = kvb.at[zs, g, c * 256 : c * 256 + 256, :]
+        return rc(ref, ref, rsem.at[way, i, c], rrsem.at[way, i, c], (zr, zl)[way])
 
     def wcopy(t):
         return rc(
@@ -209,6 +210,35 @@
             wobuf.at[pl.ds(pl.multiple_of(yh * 1024 + t * 128, 128), 128), :],
             wosem.at[t], worsem.at[t], part,
         )
+
+    def when(cond):
+        if isinstance(cond, bool):
+            return (lambda f: f()) if cond else (lambda f: None)
+        return pl.when(cond)
+
+    def forward(c, i):
+        z_r, g_r, z_l, g_l = slots(i)
+        ring(0, i, c, z_r, g_r).wait_recv()
+
+        @when(i <= 4)
+        def _():
+            ring(0, i + 2, c, z_r, g_r).start()
+
+        ring(1, i, c, z_l, g_l).wait_recv()
+
+        @when(i <= 3)
+        def _():
+            ring(1, i + 2, c, z_l, g_l).start()
+
+        @when(i == 5)
+        def _():
+            ring(1, i + 1, c, z_l, g_l).start()
+
+    def keys_values(c):
+        for g in range(2):
+            kvb[z, g, c * 256 : c * 256 + 256, :] = whole(c, g).astype(BF16)
+            for way in (0, 1):
+                go("all", ring, way, g, c, z, g)
 
     pass_on(0)
     for w in wloads:
@@ -219,6 +249,7 @@
     pass_on(1)
     from_sib(1)
     pair_up(1, product(1, 1), product(1, 2))
+    keys_values(0)
     qfull = product(1, 0)
     for h in range(2):
         lt, rt = qf[:, h * 128 : h * 128 + 128], qfull[:, h * 128 : h * 128 + 128]
@@ -232,44 +263,23 @@
     acc[...] = jnp.zeros_like(acc)
     for t in range(8):
         go("all", wcopy, t)
-    for g in range(2):
-        for c in range(2):
-            kvb[z, g, c * 256 : c * 256 + 256, :] = whole(c, g).astype(BF16)
-        for way in (0, 1):
-            go("all", ring, way, g, z, g)
+    forward(0, 0)
+    forward(0, 1)
+    keys_values(1)
+    forward(0, 2)
     for g in range(2):
         q = whole(2, g) * qscale
         qb[g * 512 : g * 512 + 256, :] = jnp.where(low, q, 0.0).astype(BF16)
         qb[g * 512 + 256 : g * 512 + 512, :] = jnp.where(low, pltpu.roll(q, 64, 1), 0.0).astype(BF16)
 
-    def step(t, carry):
-        i = t - 1
-        z_r, g_r, z_l, g_l = slots(i)
-
-        @pl.when(t >= 1)
-        def _():
-            ring(0, i, z_r, g_r).wait_recv()
-
-            @pl.when(i <= 4)
-            def _():
-                ring(0, i + 2, z_r, g_r).start()
-
-            ring(1, i, z_l, g_l).wait_recv()
-
-            @pl.when(i <= 3)
-            def _():
-                ring(1, i + 2, z_l, g_l).start()
-
-            @pl.when(i == 5)
-            def _():
-                ring(1, i + 1, z_l, g_l).start()
-
+    def attend(z_r, g_r, z_l, g_l, r0, rows):
+        r = slice(r0, r0 + rows)
         kv = jnp.concatenate([kvb[z_r, g_r], kvb[z_l, g_l]], axis=0)
         lane = lax.broadcasted_iota(jnp.int32, kv.shape, 1)
         vals = jnp.where(lane < 64, jnp.ones_like(kv), kv)
-        s = dot_t(qb[...], kv)
+        s = dot_t(qb[r, :], kv)
         n = s.shape[1] // 128
-        old = mst[...]
+        old = mst[r, :]
         mx = s[:, :128]
         for j in range(1, n):
             mx = jnp.maximum(mx, s[:, j * 128 : (j + 1) * 128])
@@ -277,14 +287,31 @@
         w = jnp.concatenate(
             [jnp.exp2(s[:, j * 128 : (j + 1) * 128] - new).astype(BF16) for j in range(n)], axis=1
         )
-        acc[...] = acc[...] * jnp.exp2(old - new) + dot(w, vals)
-        mst[...] = new
+        acc[r, :] = acc[r, :] * jnp.exp2(old - new) + dot(w, vals)
+        mst[r, :] = new
+
+    def step(t, carry):
+        i = t - 1
+        z_r, g_r, z_l, g_l = slots(i)
+
+        @pl.when(t >= 1)
+        def _():
+            forward(1, i)
+
+            @pl.when(i <= 6 - AHEAD)
+            def _():
+                forward(0, i + AHEAD)
+
+        attend(z_r, g_r, z_l, g_l, 0, 1024)
         return carry
 
-    lax.fori_loop(0, 8, step, 0)
+    lax.fori_loop(0, 7, step, 0)
+    last = slots(6)
+    forward(1, 6)
     for way in (0, 1):
         for i in range(2, 7):
-            sent["all"].append((ring, (way, i, z, 0)))
+            for c in range(2):
+                sent["all"].append((ring, (way, i, c, z, 0)))
 
     early = {who: pending[:] for who, pending in sent.items()}
     for pending in sent.values():
@@ -294,7 +321,9 @@
     def hand(b, i):
         return rc(ao.at[b], att.at[col, y], fsem.at[b, i], arsem.at[col, y], at(b, i))
 
-    for b in (3, 1, 2, 0):
+    for b in (3, 2, 1, 0):
+        if b % 2 == 1:
+            attend(*last, (b // 2) * 512, 512)
         g, a = b // 2, ys[b][1]
         r0 = pl.multiple_of(g * 512 + a * 128, 128)
         t0 = acc[pl.ds(r0, 128), :]
@@ -363,7 +392,7 @@
         pltpu.VMEM((8, 4, 128, 128), BF16),
         pltpu.VMEM((4, 256, 512), BF16),
         dma((4,)), dma((2,)), dma((2, 4)), dma((2, 4, 2)), dma((2, 2, 2)), dma((2, 4, 2)),
-        dma((3, 4)), dma((3, 4)), dma((2, 7)), dma((2, 7)),
+        dma((3, 4)), dma((3, 4)), dma((2, 7, 2)), dma((2, 7, 2)),
         dma((8,)), dma((8,)), dma((4, 4)), dma((8, 4)), dma((4,)), dma((8,)),
     ]
     return pl.pallas_call(

time: 68.2 us -> 66.8 us (0.979)
  Pallas kernels: 67.4 us -> 66 us
    pallas_call x1, Pallas kernels: 67.4 us -> 66 us  [on_device(): pl.pallas_call(kernel, out_shape=jax.ShapeDtypeStruct((256, 512), BF16),...]
where the time goes in v1:
time: 66.8 us; the launch traced here: 66.7 us
  Pallas kernels  66 us (99%)
  local copies, waits for them, and re-layouts  0.71 us (1%)
    pallas_call x1, Pallas kernels, on_device(): pl.pallas_call(kernel, out_shape=jax.ShapeDtypeStruct((256, 512), BF16),...  66 us

profile of v1, /device:TPU:1, one launch (start us, length us, event | category | flops | bytes accessed | tf_op | source)
XLA Modules:
  0.0 66.7 jit_solution(9488759776013989671)
XLA Ops:
  0.0 66.0 %shard_map.55 = bf16[256,512]{1,0:T(8,128)(2,1)S(1)} custom-call(bf16[256,512]{1,0:T(8,128)(2,1)} %tok.1, bf16[2048,256]{1,0:T(8,128)(2,1)} %wq.1, bf16[2048,256]{1,0:T(8,128)(2,1)} %wk.1, bf16[2048,256]{1,0:T(8,128)(2,1)} %wv.1, bf16[1024,512]{1,0:T(8,128)(2,1)} %wo.1), custom_call_target="tpu_custom_call" | custom-call | tf_op jit(solution)/shard_map/pallas_call | solution.py:398
  66.0 0.7 %copy.7 = bf16[256,512]{1,0:T(8,128)(2,1)} copy(bf16[256,512]{1,0:T(8,128)(2,1)S(1)} %shard_map.55) | data formatting | bytes 524288

commit v2 on v1

--- a/solution.py
+++ b/solution.py
@@ -344,32 +344,39 @@
     finish()
     sent["all"][:] = handed
 
-    def acopy(q):
-        c8 = xs[q] * 2 + k
-        return rc(att.at[c8], att.at[c8], asib.at[q], asibr.at[c8], sib)
+    def acopy(q, b):
+        place = xs[q] * 2 + k, ys[b][1] * 2 + ys[b][0]
+        return rc(att.at[place], att.at[place], asib.at[q, b], asibr.at[place], sib)
 
     for q in range(4):
         for b in range(4):
             if q + b > 0:
-                ref = att.at[xs[q] * 2 + k, ys[b][1] * 2 + ys[b][0]]
-                rc(ref, ref, fsem.at[0, 0], arsem.at[xs[q] * 2 + k, ys[b][1] * 2 + ys[b][0]], sib).wait_recv()
-        go("all", acopy, q)
+                place = xs[q] * 2 + k, ys[b][1] * 2 + ys[b][0]
+                ref = att.at[place]
+                rc(ref, ref, fsem.at[0, 0], arsem.at[place], sib).wait_recv()
+            go("all", acopy, q, b)
     for t in range(8):
         there = pl.ds(pl.multiple_of((1 - yh) * 1024 + t * 128, 128), 128)
         rc(wobuf.at[there, :], wobuf.at[there, :], wosem.at[t], worsem.at[t], sib).wait_recv()
 
-    total = None
+    def mix(q, core, n):
+        for p in range(2):
+            b0, b1 = att[xs[q] * 2 + core, 2 * p], att[xs[q] * 2 + core, 2 * p + 1]
+            c0 = p * 128
+            lhs[n, q, 0:128, c0 : c0 + 128] = jnp.concatenate([b0[:, :64], b1[:, :64]], axis=1)
+            lhs[n, q, 128:256, c0 : c0 + 128] = jnp.concatenate([b0[:, 64:], b1[:, 64:]], axis=1)
+        first = pl.multiple_of(xs[q] * 512 + core * 256, 256)
+        return dot(lhs[n, q], wobuf[pl.ds(first, 256), :])
+
+    total = mix(0, k, 0)
+    for q in range(1, 4):
+        total += mix(q, k, 0)
     for q in range(4):
-        c8 = xs[q] * 2 + 1 - k
-        rc(att.at[c8], att.at[c8], asib.at[q], asibr.at[c8], sib).wait_recv()
-        for kk in range(2):
-            for p in range(2):
-                b0, b1 = att[xs[q] * 2 + kk, 2 * p], att[xs[q] * 2 + kk, 2 * p + 1]
-                c0 = kk * 256 + p * 128
-                lhs[q, 0:128, c0 : c0 + 128] = jnp.concatenate([b0[:, :64], b1[:, :64]], axis=1)
-                lhs[q, 128:256, c0 : c0 + 128] = jnp.concatenate([b0[:, 64:], b1[:, 64:]], axis=1)
-        term = dot(lhs[q], wobuf[pl.ds(pl.multiple_of(xs[q] * 512, 512), 512), :])
-        total = term if total is None else total + term
+        for b in range(4):
+            place = xs[q] * 2 + 1 - k, ys[b][1] * 2 + ys[b][0]
+            ref = att.at[place]
+            rc(ref, ref, asib.at[q, b], asibr.at[place], sib).wait_recv()
+        total += mix(q, 1 - k, 1)
     out[...] = total.astype(BF16)
     finish()
 
@@ -390,10 +397,10 @@
         pltpu.VMEM((1024, 128), F32),
         pltpu.VMEM((4, 128, 128), BF16),
         pltpu.VMEM((8, 4, 128, 128), BF16),
-        pltpu.VMEM((4, 256, 512), BF16),
+        pltpu.VMEM((2, 4, 256, 256), BF16),
         dma((4,)), dma((2,)), dma((2, 4)), dma((2, 4, 2)), dma((2, 2, 2)), dma((2, 4, 2)),
         dma((3, 4)), dma((3, 4)), dma((2, 7, 2)), dma((2, 7, 2)),
-        dma((8,)), dma((8,)), dma((4, 4)), dma((8, 4)), dma((4,)), dma((8,)),
+        dma((8,)), dma((8,)), dma((4, 4)), dma((8, 4)), dma((4, 4)), dma((8, 4)),
     ]
     return pl.pallas_call(
         kernel,

time: 66.8 us -> 66.8 us (level)
  no operation moved by 1% of the time
where the time goes in v2:
time: 66.8 us; the launch traced here: 66.7 us
  Pallas kernels  66 us (99%)
  local copies, waits for them, and re-layouts  0.71 us (1%)
    pallas_call x1, Pallas kernels, on_device(): pl.pallas_call(kernel, out_shape=jax.ShapeDtypeStruct((256, 512), BF16),...  66 us

profile of v2, /device:TPU:1, one launch (start us, length us, event | category | flops | bytes accessed | tf_op | source)
XLA Modules:
  0.0 66.7 jit_solution(5451915720757374247)
XLA Ops:
  0.0 66.0 %shard_map.55 = bf16[256,512]{1,0:T(8,128)(2,1)S(1)} custom-call(bf16[256,512]{1,0:T(8,128)(2,1)} %tok.1, bf16[2048,256]{1,0:T(8,128)(2,1)} %wq.1, bf16[2048,256]{1,0:T(8,128)(2,1)} %wk.1, bf16[2048,256]{1,0:T(8,128)(2,1)} %wv.1, bf16[1024,512]{1,0:T(8,128)(2,1)} %wo.1), custom_call_target="tpu_custom_call" | custom-call | tf_op jit(solution)/shard_map/pallas_call | solution.py:405
  66.0 0.7 %copy.7 = bf16[256,512]{1,0:T(8,128)(2,1)} copy(bf16[256,512]{1,0:T(8,128)(2,1)S(1)} %shard_map.55) | data formatting | bytes 524288

commit v3 on v1

--- a/solution.py
+++ b/solution.py
@@ -261,7 +261,7 @@
         go("all", pcopy, 2, b)
     mst[...] = jnp.full_like(mst, -1e30)
     acc[...] = jnp.zeros_like(acc)
-    for t in range(8):
+    for t in range(4):
         go("all", wcopy, t)
     forward(0, 0)
     forward(0, 1)
@@ -271,6 +271,9 @@
         q = whole(2, g) * qscale
         qb[g * 512 : g * 512 + 256, :] = jnp.where(low, q, 0.0).astype(BF16)
         qb[g * 512 + 256 : g * 512 + 512, :] = jnp.where(low, pltpu.roll(q, 64, 1), 0.0).astype(BF16)
+
+    for t in range(4, 8):
+        go("all", wcopy, t)
 
     def attend(z_r, g_r, z_l, g_l, r0, rows):
         r = slice(r0, r0 + rows)

time: 66.8 us -> 66.8 us (level)
  no operation moved by 1% of the time
where the time goes in v3:
time: 66.8 us; the launch traced here: 66.7 us
  Pallas kernels  66 us (99%)
  local copies, waits for them, and re-layouts  0.71 us (1%)
    pallas_call x1, Pallas kernels, on_device(): pl.pallas_call(kernel, out_shape=jax.ShapeDtypeStruct((256, 512), BF16),...  66 us

profile of v3, /device:TPU:1, one launch (start us, length us, event | category | flops | bytes accessed | tf_op | source)
XLA Modules:
  0.0 66.7 jit_solution(9530810892385761887)
XLA Ops:
  0.0 66.0 %shard_map.55 = bf16[256,512]{1,0:T(8,128)(2,1)S(1)} custom-call(bf16[256,512]{1,0:T(8,128)(2,1)} %tok.1, bf16[2048,256]{1,0:T(8,128)(2,1)} %wq.1, bf16[2048,256]{1,0:T(8,128)(2,1)} %wk.1, bf16[2048,256]{1,0:T(8,128)(2,1)} %wv.1, bf16[1024,512]{1,0:T(8,128)(2,1)} %wo.1), custom_call_target="tpu_custom_call" | custom-call | tf_op jit(solution)/shard_map/pallas_call | solution.py:401
  66.0 0.7 %copy.7 = bf16[256,512]{1,0:T(8,128)(2,1)} copy(bf16[256,512]{1,0:T(8,128)(2,1)S(1)} %shard_map.55) | data formatting | bytes 524288
